TPU v7x, 256 devices: a whole 4x4x8 slice. The times are simulated.
256 devices in a mesh: tm: 64 (over x, z, y_lo), sx: 2 (over core), sy: 2 (over y_hi).
Axes of the slice: x: 4, y: 4 (y_hi: 2, y_lo: 2; y = y_hi * 2 + y_lo), z: 8, core: 2. Of those that a mesh axis runs over, the one named last changes fastest.
Arguments:
- initial_states: float32 [64, 8, 64, 256], P('tm', None, 'sx', 'sy'), may hold values from -6 to 6
- coarse_decay: float32 [64, 8, 64, 256], P('tm', None, 'sx', 'sy'), may hold values from 0 to 1, as said below
- power_map: float32 [8, 64, 256], P(None, 'sx', 'sy'), may hold values from 0.5 to 2
- power_mask: int32 [64, 4, 8], P('tm'), may hold values 0 or 1
- region_ids: int32 [8, 8], replicated, may hold values from 0 to 3
- region_conductivity: float32 [4], replicated, may hold values from 0.4 to 2.5
Outputs:
- cycle_states: float32 [64, 8, 64, 256], P('tm', None, 'sx', 'sy')
- jump_field: float32 [64, 8, 64, 256], P('tm', None, 'sx', 'sy')
Inputs may be any that keep to these rules, and one draw needn't show every extreme that they name: `coarse_decay`: every entry lies between 0 and 1, and for every cell the product of its 64 factors is at most one half.
All inputs are finite; a program needn't handle non-finite values. No bound on the sum of `power_mask` on one device may be relied on, other than what follows from the above.
Results may differ from a plain program's by a relative error of at most 0.0001.
Values sent between devices are 32-bit elements; how exact they have to be, the bound alone decides.
No kernel may reach another device: no remote copies, remote signals or barrier semaphores. Data moves between devices by JAX's collectives and lax.ppermute only.
A program may use at most 128 MiB of HBM per device.

v0:
```python
import jax
import jax.numpy as jnp
from jax import lax
from jax.sharding import PartitionSpec as P

RB = 8
REGIONS = 4
FSTEPS = 4
SWEEPS = 3
ITERS = 2
grid_xy = 1.0
grid_z = 0.5
sink_gain = 0.5
source_gain = 0.5
cond_slope = 0.25
joule_slope = 0.3


def padded_2(x, sides, width):
    for axis, dim in sides:
        peers, length = (lax.axis_size(axis), x.shape[dim])
        up = [(i, (i + 1) % peers) for i in range(peers - 1)]
        down = [(j, i) for i, j in up]
        last = lax.slice_in_dim(x, length - width, length, axis=dim)
        initial = lax.slice_in_dim(x, 0, width, axis=dim)
        before = lax.ppermute(last, axis, up)
        after = lax.ppermute(initial, axis, down)
        x = jnp.concatenate([before, x, after], axis=dim)
    return x


def entering(x, axis, combine, identity):
    peers, here = (lax.axis_size(axis), lax.axis_index(axis))
    everything = jax.tree.map(lambda part: lax.all_gather(part, axis), x)
    start = jax.tree.map(
        lambda part, zero: jnp.broadcast_to(jnp.asarray(zero, part.dtype), part.shape), x, identity
    )

    def step(k, before):
        reached = k < here
        new = combine(before, jax.tree.map(lambda part: part[k], everything))
        return jax.tree.map(lambda a, b: jnp.where(reached, a, b), new, before)

    return lax.fori_loop(0, peers, step, start)


def broadcast(x, axis, root):
    mine = lax.axis_index(axis) == root
    return lax.psum(jnp.where(mine, x, jnp.zeros_like(x)), axis)


def passed_along(block, axis, distance):
    devices = range(lax.axis_size(axis))
    route = [((i - distance) % len(devices), i) for i in devices]
    return lax.ppermute(block, axis, route)


def base_rows(region_ids, region_conductivity):
    labels = jnp.arange(REGIONS, dtype=jnp.int32)
    chosen = (region_ids[:, :, None] == labels[None, None, :]).astype(jnp.float32)
    return jnp.sum(chosen * region_conductivity[None, None, :], axis=2)


def face_weights(cond_pad, weight_scale):
    middle = cond_pad[:, 1:-1, 1:-1]
    layer_index = lax.broadcasted_iota(jnp.int32, middle.shape, 0)
    blank_layer = jnp.zeros_like(middle[:1])
    layer_above = jnp.concatenate([middle[1:], blank_layer], axis=0)
    layer_below = jnp.concatenate([blank_layer, middle[:-1]], axis=0)
    weight_west = weight_scale * (grid_xy * (0.5 * (middle + cond_pad[:, :-2, 1:-1])))
    weight_east = weight_scale * (grid_xy * (0.5 * (middle + cond_pad[:, 2:, 1:-1])))
    weight_south = weight_scale * (grid_xy * (0.5 * (middle + cond_pad[:, 1:-1, :-2])))
    weight_north = weight_scale * (grid_xy * (0.5 * (middle + cond_pad[:, 1:-1, 2:])))
    weight_up = jnp.where(
        layer_index == middle.shape[0] - 1,
        jnp.zeros_like(middle),
        weight_scale * (grid_z * (0.5 * (middle + layer_above))),
    )
    weight_down = jnp.where(
        layer_index == 0,
        weight_scale * (sink_gain * middle),
        weight_scale * (grid_z * (0.5 * (middle + layer_below))),
    )
    denominator = 1.0 + (
        weight_west + weight_east + weight_south + weight_north + weight_down + weight_up
    )
    return (
        (weight_west, weight_east, weight_south, weight_north, weight_down, weight_up),
        denominator,
    )


def relax(padded, weights, right_side, denominator):
    weight_west, weight_east, weight_south, weight_north, weight_down, weight_up = weights
    middle = padded[:, 1:-1, 1:-1]
    blank_layer = jnp.zeros_like(middle[:1])
    layer_above = jnp.concatenate([middle[1:], blank_layer], axis=0)
    layer_below = jnp.concatenate([blank_layer, middle[:-1]], axis=0)
    summed = weight_west * padded[:, :-2, 1:-1] + weight_east * padded[:, 2:, 1:-1]
    summed = summed + weight_south * padded[:, 1:-1, :-2] + weight_north * padded[:, 1:-1, 2:]
    summed = summed + weight_down * layer_below + weight_up * layer_above
    return (right_side + summed) / denominator


def compose_forward(earlier, later):
    return (earlier[0] * later[0], later[0] * earlier[1] + later[1])


def shards(initial_states, coarse_decay, power_map, power_mask, region_ids, region_conductivity):
    tile_rows = initial_states.shape[2]
    tile_cols = initial_states.shape[3]
    block_count = region_ids.shape[1]
    row_first = lax.axis_index("sx") * tile_rows
    col_first = lax.axis_index("sy") * tile_cols
    grid_rows = tile_rows * lax.axis_size("sx")
    grid_cols = tile_cols * lax.axis_size("sy")
    per_block = base_rows(region_ids, region_conductivity)
    mask_blocks = power_mask[0].astype(jnp.float32)
    row_ids = row_first - 1 + jnp.arange(tile_rows + 2 * 1, dtype=jnp.int32)
    col_ids = col_first - 1 + jnp.arange(tile_cols + 2 * 1, dtype=jnp.int32)
    row_inside = ((row_ids >= 0) & (row_ids < grid_rows)).astype(jnp.float32)
    col_inside = ((col_ids >= 0) & (col_ids < grid_cols)).astype(jnp.float32)
    block_of = jnp.clip(row_ids // RB, 0, block_count - 1)
    block_hit = (block_of[:, None] == jnp.arange(block_count, dtype=jnp.int32)[None, :]).astype(
        jnp.float32
    )
    base_cond = jnp.sum(per_block[:, None, :] * block_hit[None, :, :], axis=2)
    mask_rows = jnp.sum(mask_blocks[:, None, :] * block_hit[None, :, :], axis=2)
    inside = row_inside[None, :, None] * col_inside[None, None, :]
    decay_rate = coarse_decay[0]
    states = initial_states[0]
    jump_field = jnp.zeros_like(states)
    for round_index in range(ITERS):
        current = states
        previous = states
        for substep in range(FSTEPS):
            if substep == 0:
                coef_now, coef_old, weight_scale = (1.0, 0.0, 1.0)
            else:
                coef_now, coef_old, weight_scale = (4.0 / 3.0, -1.0 / 3.0, 2.0 / 3.0)
            iterate = current
            for sweep_index in range(SWEEPS):
                padded = padded_2(iterate, (("sx", 1), ("sy", 2)), 1)
                if sweep_index == 0:
                    conductance = (
                        base_cond[:, :, None] * (1.0 - cond_slope * jnp.tanh(padded)) * inside
                    )
                    weights, denominator = face_weights(conductance, weight_scale)
                    heat_source = (
                        source_gain
                        * mask_rows[substep][1:-1][None, :, None]
                        * power_map
                        * (1.0 + joule_slope * jnp.tanh(current))
                    )
                    right_side = (
                        coef_now * current + coef_old * previous + weight_scale * heat_source
                    )
                iterate = relax(padded, weights, right_side, denominator)
            previous = current
            current = iterate
        if round_index == ITERS - 1:
            following = passed_along(states, "tm", -1)
            jump_field = current - following
        offset = current - decay_rate * states
        unit_map = jnp.ones_like(decay_rate)
        zero_map = jnp.zeros_like(decay_rate)
        scale_pre, shift_pre = entering(
            (decay_rate, offset), "tm", compose_forward, (unit_map, zero_map)
        )
        scale_incl = scale_pre * decay_rate
        shift_incl = decay_rate * shift_pre + offset
        scale_total = broadcast(scale_incl, "tm", lax.axis_size("tm") - 1)
        shift_total = broadcast(shift_incl, "tm", lax.axis_size("tm") - 1)
        first_state = shift_total / (1.0 - scale_total)
        states = scale_pre * first_state + shift_pre
    return (states[None], jump_field[None])


def solution(mesh):
    return jax.shard_map(
        shards,
        mesh=mesh,
        in_specs=(
            P("tm", None, "sx", "sy"),
            P("tm", None, "sx", "sy"),
            P(None, "sx", "sy"),
            P("tm", None, None),
            P(),
            P(),
        ),
        out_specs=(P("tm", None, "sx", "sy"), P("tm", None, "sx", "sy")),
        check_vma=False,
    )
```

profile of v0, /device:TPU:16, one launch (start us, length us, event | category | flops | bytes accessed | tf_op | source)
XLA Modules:
  0.0 2389.5 jit_solution(18325061548936301741)
XLA Ops:
  17.0 6.1 collective-permute-start.3
  23.1 5.6 collective-permute-done.2
  28.7 1.9 collective-permute-done.3
  36.6 1.7 collective-permute-done.5
  39.8 6.3 collective-permute-start.7
  46.1 7.7 collective-permute-done.6
  57.4 1.7 collective-permute-done.9
  60.6 6.6 collective-permute-start.11
  67.2 7.3 collective-permute-done.10
  78.8 1.7 collective-permute-done.13
  82.0 6.5 collective-permute-start.15
  88.5 7.3 collective-permute-done.14
  100.1 1.7 collective-permute-done.17
  103.3 6.3 collective-permute-start.19
  109.6 8.0 collective-permute-done.18
  121.2 1.7 collective-permute-done.21
  124.4 6.1 collective-permute-start.23
  130.5 7.4 collective-permute-done.22
  141.9 1.7 collective-permute-done.25
  145.1 6.5 collective-permute-start.27
  151.6 7.8 collective-permute-done.26
  160.2 2.3 collective-permute-start.28
  167.0 6.1 collective-permute-start.31
  173.1 7.0 collective-permute-done.30
  187.4 6.1 collective-permute-start.35
  193.5 7.8 collective-permute-done.34
  207.9 6.3 collective-permute-start.39
  214.3 8.1 collective-permute-done.38
  229.1 6.1 collective-permute-start.43
  235.2 7.2 collective-permute-done.42
  249.5 6.4 collective-permute-start.47
  256.0 7.6 collective-permute-done.46
  265.6 62.2 %all-gather.6.cloned.1.call-done = f32[64,8,32,128]{3,2,1,0:T(8,128)} async-done(((f32[1,8,32,128]{3,2,1,0:T(8,128)}), f32[64,8,32,128]{3,2,1,0:T(8,128)}) %all-gather.6.cloned.1.call-update) | async-done | bytes 8388624 | tf_op jit(solution)/shard_map/all_gather | solution.py:34
  327.9 313.3 %all-gather.8.cloned.1.call-done = f32[512,32,128]{2,1,0:T(8,128)} async-done(((f32[8,32,128]{2,1,0:T(8,128)}), f32[512,32,128]{2,1,0:T(8,128)}) %all-gather.8.cloned.1.call-update) | async-done | bytes 8388624 | tf_op jit(solution)/shard_map/all_gather | solution.py:34
  641.2 70.5 %while.32 = (s32[]{:T(128)}, f32[8,32,128]{2,1,0:T(8,128)S(1)}, f32[8,32,128]{2,1,0:T(8,128)S(1)}, s32[]{:T(128)}, f32[64,8,32,128]{3,2,1,0:T(8,128)}, /*index=5*/f32[64,8,32,128]{3,2,1,0:T(8,128)}, s32[]{:T(128)}, s32[]{:T(128)}) while((s32[]{:T(128)}, f32[8,32,128]{2,1,0:T(8,128)S(1)}, f32[8,32,128]{2,1,0:T(8,128)S(1)}, ...), condition=%wide.region_4.5_spmd.clone, body=%wide.region_3.4_spmd.clone.sunk | while | flops 229380 | bytes 786541 | solution.py:44
  713.5 545.3 %all-reduce.71.cloned.1.call-done = (f32[8,32,128]{2,1,0:T(8,128)}, f32[8,32,128]{2,1,0:T(8,128)}) async-done(((f32[8,32,128]{2,1,0:T(8,128)}, f32[8,32,128]{2,1,0:T(8,128)}), (f32[8,32,128]{2,1,0:T(8,128)}, f32[8,32,128]{2,1,0:T(8,128)})) %all-reduce.71.cloned.1.call-update) | async-done | bytes 262160 | tf_op jit(solution)/shard_map/psum | solution.py:49
  1265.8 6.1 collective-permute-start.51
  1271.9 2.1 collective-permute-done.50
  1281.9 6.1 collective-permute-start.55
  1288.0 2.4 collective-permute-done.54
  1297.8 6.1 collective-permute-start.59
  1303.9 2.4 collective-permute-done.58
  1313.7 6.1 collective-permute-start.63
  1319.8 2.4 collective-permute-done.62
  1330.0 6.1 collective-permute-start.67
  1336.1 2.4 collective-permute-done.66
  1345.9 6.1 collective-permute-start.71
  1352.0 2.4 collective-permute-done.70
  1361.7 6.1 collective-permute-start.75
  1367.8 2.4 collective-permute-done.74
  1378.0 6.1 collective-permute-start.79
  1384.1 2.4 collective-permute-done.78
  1393.9 6.1 collective-permute-start.83
  1400.0 2.4 collective-permute-done.82
  1409.7 6.1 collective-permute-start.87
  1415.8 2.4 collective-permute-done.86
  1426.1 6.1 collective-permute-start.91
  1432.2 2.4 collective-permute-done.90
  1438.7 2.5 collective-permute-start.96
  1442.6 6.1 collective-permute-start.95
  1448.7 2.9 collective-permute-done.94
  1454.7 309.4 %all-gather.10.cloned.1.call-done = f32[512,32,128]{2,1,0:T(8,128)} async-done(((f32[8,32,128]{2,1,0:T(8,128)}), f32[512,32,128]{2,1,0:T(8,128)}) %all-gather.10.cloned.1.call-update) | async-done | bytes 8388624 | tf_op jit(solution)/shard_map/all_gather | solution.py:34
  1764.0 70.0 %while.33 = (s32[]{:T(128)}, f32[8,32,128]{2,1,0:T(8,128)S(1)}, f32[8,32,128]{2,1,0:T(8,128)S(1)}, s32[]{:T(128)}, f32[64,8,32,128]{3,2,1,0:T(8,128)}, /*index=5*/f32[64,8,32,128]{3,2,1,0:T(8,128)}, s32[]{:T(128)}, s32[]{:T(128)}) while((s32[]{:T(128)}, f32[8,32,128]{2,1,0:T(8,128)S(1)}, f32[8,32,128]{2,1,0:T(8,128)S(1)}, ...), condition=%wide.region_8.9_spmd.clone, body=%wide.region_7.8_spmd.clone.sunk | while | flops 229380 | bytes 786541 | solution.py:44
  1835.8 545.5 %all-reduce.69.cloned.1.call-done = (f32[8,32,128]{2,1,0:T(8,128)}, f32[8,32,128]{2,1,0:T(8,128)}) async-done(((f32[8,32,128]{2,1,0:T(8,128)}, f32[8,32,128]{2,1,0:T(8,128)}), (f32[8,32,128]{2,1,0:T(8,128)}, f32[8,32,128]{2,1,0:T(8,128)})) %all-reduce.69.cloned.1.call-update) | async-done | bytes 262160 | tf_op jit(solution)/shard_map/psum | solution.py:49
  (437 shorter events, 312.1 us)
Async XLA Ops:
  7.2 320.7 %all-gather.6.cloned.1.call-start = ((), (), s32[]{:S(2)}) async-start(), calls=%async_computation | async-start | bytes 8519680 | tf_op jit(solution)/shard_map/all_gather | solution.py:34
  7.9 633.3 %all-gather.8.cloned.1.call-start = ((), (), s32[]{:S(2)}) async-start(), calls=%async_computation.1 | async-start | bytes 8519680 | tf_op jit(solution)/shard_map/all_gather | solution.py:34
  8.8 5.9 collective-permute-start
  10.5 4.2 collective-permute-start.1
  15.7 13.0 collective-permute-start.2
  17.0 13.6 collective-permute-start.3
  35.3 3.1 collective-permute-start.5
  38.5 15.3 collective-permute-start.6
  39.8 14.7 collective-permute-start.7
  56.1 3.1 collective-permute-start.9
  59.3 15.2 collective-permute-start.10
  60.6 15.2 collective-permute-start.11
  77.5 3.1 collective-permute-start.13
  80.7 15.1 collective-permute-start.14
  82.0 14.4 collective-permute-start.15
  98.8 3.1 collective-permute-start.17
  102.0 15.6 collective-permute-start.18
  103.3 14.7 collective-permute-start.19
  119.9 3.1 collective-permute-start.21
  123.1 14.8 collective-permute-start.22
  124.4 14.4 collective-permute-start.23
  143.8 15.6 collective-permute-start.26
  145.1 14.3 collective-permute-start.27
  160.2 3.6 collective-permute-start.28
  165.7 14.4 collective-permute-start.30
  167.0 14.3 collective-permute-start.31
  186.1 15.2 collective-permute-start.34
  187.4 14.3 collective-permute-start.35
  206.6 15.8 collective-permute-start.38
  207.9 14.5 collective-permute-start.39
  227.8 14.6 collective-permute-start.42
  229.1 14.3 collective-permute-start.43
  248.2 15.4 collective-permute-start.46
  249.5 15.0 collective-permute-start.47
  265.6 993.2 %all-reduce.71.cloned.1.call-start = ((), (), s32[]{:S(2)}) async-start(), calls=%async_computation.4 | async-start | bytes 524288 | tf_op jit(solution)/shard_map/psum | solution.py:49
  713.4 1050.6 %all-gather.10.cloned.1.call-start = ((), (), s32[]{:S(2)}) async-start(), calls=%async_computation.2 | async-start | bytes 8519680 | tf_op jit(solution)/shard_map/all_gather | solution.py:34
  1264.3 9.7 collective-permute-start.50
  1265.8 9.6 collective-permute-start.51
  1280.6 9.8 collective-permute-start.54
  1281.9 9.7 collective-permute-start.55
  1296.5 9.8 collective-permute-start.58
  1297.8 9.7 collective-permute-start.59
  1312.4 9.8 collective-permute-start.62
  1313.7 9.7 collective-permute-start.63
  1328.7 9.8 collective-permute-start.66
  1330.0 9.7 collective-permute-start.67
  1344.6 9.8 collective-permute-start.70
  1345.9 9.7 collective-permute-start.71
  1360.4 9.8 collective-permute-start.74
  1361.7 9.7 collective-permute-start.75
  1376.7 9.8 collective-permute-start.78
  1378.0 9.7 collective-permute-start.79
  1392.6 9.8 collective-permute-start.82
  1393.9 9.7 collective-permute-start.83
  1408.4 9.8 collective-permute-start.86
  1409.7 9.7 collective-permute-start.87
  1424.8 9.8 collective-permute-start.90
  1426.1 9.7 collective-permute-start.91
  1436.1 5.1 collective-permute-start.92
  1437.4 3.8 collective-permute-start.93
  1438.7 14.2 collective-permute-start.96
  1441.3 10.3 collective-permute-start.94
  1442.6 10.2 collective-permute-start.95
  1454.6 926.7 %all-reduce.69.cloned.1.call-start = ((), (), s32[]{:S(2)}) async-start(), calls=%async_computation.3 | async-start | bytes 524288 | tf_op jit(solution)/shard_map/psum | solution.py:49
  (41 other events, 391.1 us)
Sparse Core Ops, SparseCore 0:
  9.8 318.0 all-gather.5
  330.2 310.9 all-gather.7
  713.5 545.1 all-reduce.70
  1454.7 309.2 all-gather.9
  1835.9 545.3 all-reduce.68
where the time goes:
time: 2390 us
  waiting for transfers between devices  1960 us (82%)
  starting transfers between devices  246 us (10%)
  other arithmetic  163 us (7%)
    psum x2, waiting for transfers between devices, broadcast(): return lax.psum(jnp.where(mine, x, jnp.zeros_like(x)), axis)  1090 us
    all_gather x3, waiting for transfers between devices, entering(): everything = jax.tree.map(lambda part: lax.all_gather(part, axis), x)  685 us
    ppermute x48, starting transfers between devices, padded_2(): after = lax.ppermute(initial, axis, down)  179 us
    select_n x128, other arithmetic, step(): return jax.tree.map(lambda a, b: jnp.where(reached, a, b), new, before)  138 us
    ppermute x48, waiting for transfers between devices, padded_2(): before = lax.ppermute(last, axis, up)  118 us
    ppermute x48, starting transfers between devices, padded_2(): before = lax.ppermute(last, axis, up)  64.5 us
    ppermute x48, waiting for transfers between devices, padded_2(): after = lax.ppermute(initial, axis, down)  62 us
  transfers between devices with their start and end apart: 102, of which 73 were waited for; matrix products, arithmetic and copies ran while one was open for 1% of the time, Pallas kernels for 0%

commit v1 on v0

--- a/solution.py
+++ b/solution.py
@@ -46,7 +46,7 @@
 
 def broadcast(x, axis, root):
     mine = lax.axis_index(axis) == root
-    return lax.psum(jnp.where(mine, x, jnp.zeros_like(x)), axis)
+    return jnp.sum(lax.all_gather(jnp.where(mine, x, jnp.zeros_like(x)), axis), axis=0)
 
 
 def passed_along(block, axis, distance):

time: 2390 us -> 2560 us (1.071)
  waiting for transfers between devices: 1960 us -> 2110 us
    all_gather x0 -> x4, waiting for transfers between devices: none -> 1240 us  [broadcast(): lax.all_gather(jnp.where(mine, x, jnp.zeros_like(x)), axis)]
    psum x2 -> x0, waiting for transfers between devices: 1090 us -> none  [broadcast(): return lax.psum(jnp.where(mine, x, jnp.zeros_like(x)), axis)]
  transfers between devices with their start and end apart: 102 -> 104, of which waited for: 73 -> 74; matrix products, arithmetic and copies ran while one was open for 1% -> 1% of each run, Pallas kernels for 0% -> 0%
where the time goes in v1:
time: 2560 us; the launch traced here: 2550 us
  waiting for transfers between devices  2110 us (82%)
  starting transfers between devices  247 us (10%)
  other arithmetic  177 us (7%)
    all_gather x4, waiting for transfers between devices, broadcast(): lax.all_gather(jnp.where(mine, x, jnp.zeros_like(x)), axis)  1240 us
    all_gather x3, waiting for transfers between devices, entering(): everything = jax.tree.map(lambda part: lax.all_gather(part, axis), x)  687 us
    ppermute x48, starting transfers between devices, padded_2(): after = lax.ppermute(initial, axis, down)  178 us
    select_n x128, other arithmetic, step(): return jax.tree.map(lambda a, b: jnp.where(reached, a, b), new, before)  137 us
    ppermute x48, waiting for transfers between devices, padded_2(): before = lax.ppermute(last, axis, up)  120 us
    ppermute x48, starting transfers between devices, padded_2(): before = lax.ppermute(last, axis, up)  65.3 us
    ppermute x48, waiting for transfers between devices, padded_2(): after = lax.ppermute(initial, axis, down)  58.1 us
  transfers between devices with their start and end apart: 104, of which 74 were waited for; matrix products, arithmetic and copies ran while one was open for 1% of the time, Pallas kernels for 0%

profile of v1, /device:TPU:16, one launch (start us, length us, event | category | flops | bytes accessed | tf_op | source)
XLA Modules:
  0.0 2554.6 jit_solution(3092602164809584668)
XLA Ops:
  17.0 6.1 collective-permute-start.3
  23.1 5.6 collective-permute-done.2
  39.7 6.3 collective-permute-start.7
  46.1 7.7 collective-permute-done.6
  60.6 6.6 collective-permute-start.11
  67.3 7.4 collective-permute-done.10
  81.5 6.6 collective-permute-start.15
  88.1 7.3 collective-permute-done.14
  102.8 6.1 collective-permute-start.19
  109.0 7.6 collective-permute-done.18
  123.6 6.1 collective-permute-start.23
  129.7 7.8 collective-permute-done.22
  138.0 2.1 collective-permute-start.24
  144.5 6.1 collective-permute-start.27
  150.6 7.8 collective-permute-done.26
  165.5 6.1 collective-permute-start.31
  171.6 7.8 collective-permute-done.30
  186.3 6.1 collective-permute-start.35
  192.4 7.8 collective-permute-done.34
  206.5 6.2 collective-permute-start.39
  212.8 7.7 collective-permute-done.38
  221.6 1.9 collective-permute-start.40
  228.0 6.3 collective-permute-start.43
  234.3 8.0 collective-permute-done.42
  248.8 6.1 collective-permute-start.47
  254.9 8.2 collective-permute-done.46
  264.3 63.1 %all-gather.14.cloned.1.call-done = f32[64,8,32,128]{3,2,1,0:T(8,128)} async-done(((f32[1,8,32,128]{3,2,1,0:T(8,128)}), f32[64,8,32,128]{3,2,1,0:T(8,128)}) %all-gather.14.cloned.1.call-update) | async-done | bytes 8388624 | tf_op jit(solution)/shard_map/all_gather | solution.py:34
  327.4 313.2 %all-gather.16.cloned.1.call-done = f32[512,32,128]{2,1,0:T(8,128)} async-done(((f32[8,32,128]{2,1,0:T(8,128)}), f32[512,32,128]{2,1,0:T(8,128)}) %all-gather.16.cloned.1.call-update) | async-done | bytes 8388624 | tf_op jit(solution)/shard_map/all_gather | solution.py:34
  640.6 70.1 %while.32 = (s32[]{:T(128)}, f32[8,32,128]{2,1,0:T(8,128)S(1)}, f32[8,32,128]{2,1,0:T(8,128)S(1)}, s32[]{:T(128)}, f32[64,8,32,128]{3,2,1,0:T(8,128)}, /*index=5*/f32[64,8,32,128]{3,2,1,0:T(8,128)}, s32[]{:T(128)}, s32[]{:T(128)}) while((s32[]{:T(128)}, f32[8,32,128]{2,1,0:T(8,128)S(1)}, f32[8,32,128]{2,1,0:T(8,128)S(1)}, ...), condition=%wide.region_4.5_spmd.clone, body=%wide.region_3.4_spmd.clone.sunk | while | flops 229380 | bytes 786541 | solution.py:44
  713.2 310.2 %all-gather.18.cloned.1.call-done = f32[512,32,128]{2,1,0:T(8,128)} async-done(((f32[8,32,128]{2,1,0:T(8,128)}), f32[512,32,128]{2,1,0:T(8,128)}) %all-gather.18.cloned.1.call-update) | async-done | bytes 8388624 | tf_op jit(solution)/shard_map/all_gather | solution.py:49
  1023.4 4.1 reduce_sum.66
  1027.5 309.0 %all-gather.20.cloned.1.call-done = f32[512,32,128]{2,1,0:T(8,128)} async-done(((f32[8,32,128]{2,1,0:T(8,128)}), f32[512,32,128]{2,1,0:T(8,128)}) %all-gather.20.cloned.1.call-update) | async-done | bytes 8388624 | tf_op jit(solution)/shard_map/all_gather | solution.py:49
  1336.5 4.1 reduce_sum.67
  1346.5 6.1 collective-permute-start.51
  1352.6 2.3 collective-permute-done.50
  1362.7 6.1 collective-permute-start.55
  1368.8 2.4 collective-permute-done.54
  1378.6 6.1 collective-permute-start.59
  1384.7 2.4 collective-permute-done.58
  1394.5 6.1 collective-permute-start.63
  1400.6 2.4 collective-permute-done.62
  1410.8 6.1 collective-permute-start.67
  1416.9 2.4 collective-permute-done.66
  1426.7 6.1 collective-permute-start.71
  1432.8 2.4 collective-permute-done.70
  1442.5 6.1 collective-permute-start.75
  1448.6 2.4 collective-permute-done.74
  1458.9 6.1 collective-permute-start.79
  1465.0 2.4 collective-permute-done.78
  1474.7 6.1 collective-permute-start.83
  1480.8 2.4 collective-permute-done.82
  1490.6 6.1 collective-permute-start.87
  1496.7 2.4 collective-permute-done.86
  1506.9 6.1 collective-permute-start.91
  1513.0 2.4 collective-permute-done.90
  1519.6 2.9 collective-permute-start.96
  1524.0 6.1 collective-permute-start.95
  1530.1 2.9 collective-permute-done.94
  1536.0 310.9 %all-gather.22.cloned.1.call-done = f32[512,32,128]{2,1,0:T(8,128)} async-done(((f32[8,32,128]{2,1,0:T(8,128)}), f32[512,32,128]{2,1,0:T(8,128)}) %all-gather.22.cloned.1.call-update) | async-done | bytes 8388624 | tf_op jit(solution)/shard_map/all_gather | solution.py:34
  1846.9 70.1 %while.33 = (s32[]{:T(128)}, f32[8,32,128]{2,1,0:T(8,128)S(1)}, f32[8,32,128]{2,1,0:T(8,128)S(1)}, s32[]{:T(128)}, f32[64,8,32,128]{3,2,1,0:T(8,128)}, /*index=5*/f32[64,8,32,128]{3,2,1,0:T(8,128)}, s32[]{:T(128)}, s32[]{:T(128)}) while((s32[]{:T(128)}, f32[8,32,128]{2,1,0:T(8,128)S(1)}, f32[8,32,128]{2,1,0:T(8,128)S(1)}, ...), condition=%wide.region_8.9_spmd.clone, body=%wide.region_7.8_spmd.clone.sunk | while | flops 229380 | bytes 786541 | solution.py:44
  1919.5 310.2 %all-gather.24.cloned.1.call-done = f32[512,32,128]{2,1,0:T(8,128)} async-done(((f32[8,32,128]{2,1,0:T(8,128)}), f32[512,32,128]{2,1,0:T(8,128)}) %all-gather.24.cloned.1.call-update) | async-done | bytes 8388624 | tf_op jit(solution)/shard_map/all_gather | solution.py:49
  2229.7 4.1 reduce_sum.68
  2233.8 309.1 %all-gather.26.cloned.1.call-done = f32[512,32,128]{2,1,0:T(8,128)} async-done(((f32[8,32,128]{2,1,0:T(8,128)}), f32[512,32,128]{2,1,0:T(8,128)}) %all-gather.26.cloned.1.call-update) | async-done | bytes 8388624 | tf_op jit(solution)/shard_map/all_gather | solution.py:49
  2543.0 4.1 reduce_sum.69
  (447 shorter events, 319.3 us)
Async XLA Ops:
  7.2 320.2 %all-gather.14.cloned.1.call-start = ((), (), s32[]{:S(2)}) async-start(), calls=%async_computation | async-start | bytes 8519680 | tf_op jit(solution)/shard_map/all_gather | solution.py:34
  7.9 632.7 %all-gather.16.cloned.1.call-start = ((), (), s32[]{:S(2)}) async-start(), calls=%async_computation.1 | async-start | bytes 8519680 | tf_op jit(solution)/shard_map/all_gather | solution.py:34
  8.8 5.9 collective-permute-start
  10.5 4.2 collective-permute-start.1
  15.7 13.0 collective-permute-start.2
  17.0 13.6 collective-permute-start.3
  35.2 3.1 collective-permute-start.5
  38.4 15.4 collective-permute-start.6
  39.7 14.7 collective-permute-start.7
  59.3 15.3 collective-permute-start.10
  60.6 14.7 collective-permute-start.11
  80.2 15.2 collective-permute-start.14
  81.5 14.4 collective-permute-start.15
  101.5 15.1 collective-permute-start.18
  102.8 14.1 collective-permute-start.19
  117.3 3.1 collective-permute-start.20
  122.3 15.2 collective-permute-start.22
  123.6 13.9 collective-permute-start.23
  138.0 3.4 collective-permute-start.24
  143.2 15.2 collective-permute-start.26
  144.5 14.2 collective-permute-start.27
  164.2 15.2 collective-permute-start.30
  165.5 14.6 collective-permute-start.31
  185.0 15.2 collective-permute-start.34
  186.3 14.0 collective-permute-start.35
  205.2 15.3 collective-permute-start.38
  206.5 14.2 collective-permute-start.39
  221.6 3.2 collective-permute-start.40
  226.7 15.6 collective-permute-start.42
  228.0 14.3 collective-permute-start.43
  247.5 15.6 collective-permute-start.46
  248.8 14.3 collective-permute-start.47
  264.2 759.2 %all-gather.18.cloned.1.call-start = ((), (), s32[]{:S(2)}) async-start(), calls=%async_computation.2 | async-start | bytes 8519680 | tf_op jit(solution)/shard_map/all_gather | solution.py:49
  712.4 624.1 %all-gather.20.cloned.1.call-start = ((), (), s32[]{:S(2)}) async-start(), calls=%async_computation.3 | async-start | bytes 8519680 | tf_op jit(solution)/shard_map/all_gather | solution.py:49
  713.0 1133.9 %all-gather.22.cloned.1.call-start = ((), (), s32[]{:S(2)}) async-start(), calls=%async_computation.4 | async-start | bytes 8519680 | tf_op jit(solution)/shard_map/all_gather | solution.py:34
  1345.2 9.7 collective-permute-start.50
  1346.5 9.6 collective-permute-start.51
  1361.4 9.8 collective-permute-start.54
  1362.7 9.7 collective-permute-start.55
  1377.3 9.8 collective-permute-start.58
  1378.6 9.7 collective-permute-start.59
  1393.2 9.8 collective-permute-start.62
  1394.5 9.7 collective-permute-start.63
  1409.5 9.8 collective-permute-start.66
  1410.8 9.7 collective-permute-start.67
  1425.4 9.8 collective-permute-start.70
  1426.7 9.7 collective-permute-start.71
  1441.2 9.8 collective-permute-start.74
  1442.5 9.7 collective-permute-start.75
  1457.6 9.8 collective-permute-start.78
  1458.9 9.7 collective-permute-start.79
  1473.4 9.8 collective-permute-start.82
  1474.7 9.7 collective-permute-start.83
  1489.3 9.8 collective-permute-start.86
  1490.6 9.7 collective-permute-start.87
  1505.6 9.8 collective-permute-start.90
  1506.9 9.7 collective-permute-start.91
  1517.0 5.5 collective-permute-start.92
  1518.3 4.2 collective-permute-start.93
  1519.6 14.6 collective-permute-start.96
  1522.7 10.3 collective-permute-start.94
  1524.0 10.2 collective-permute-start.95
  1536.0 693.8 %all-gather.24.cloned.1.call-start = ((), (), s32[]{:S(2)}) async-start(), calls=%async_computation.5 | async-start | bytes 8519680 | tf_op jit(solution)/shard_map/all_gather | solution.py:49
  1918.7 624.2 %all-gather.26.cloned.1.call-start = ((), (), s32[]{:S(2)}) async-start(), calls=%async_computation.6 | async-start | bytes 8519680 | tf_op jit(solution)/shard_map/all_gather | solution.py:49
  (43 other events, 396.7 us)
Sparse Core Ops, SparseCore 0:
  9.8 317.5 all-gather.13
  329.8 310.7 all-gather.15
  712.5 310.8 all-gather.17
  1025.6 310.8 all-gather.19
  1536.1 310.7 all-gather.21
  1918.9 310.8 all-gather.23
  2232.1 310.8 all-gather.25
